TPU v7x, 32 devices: a whole 2x2x4 slice. The times are simulated.
32 devices in a mesh: parts: 2 (over y), tmpl: 4 (over z), sta: 2 (over x), sub: 2 (over core).
Axes of the slice: x: 2, y: 2, z: 4, core: 2. Of those that a mesh axis runs over, the one named last changes fastest.
Arguments:
- traces: bfloat16 [16, 3, 1536], P(('tmpl', 'sta'), None, ('parts', 'sub')), parts along dimension 2
- trace_tail: bfloat16 [16, 3, 726], P(('tmpl', 'sta'), None, 'parts'), parts along dimension 2
- templates: bfloat16 [32, 3, 300], P('tmpl')
- win_lengths: int32 [32], replicated, may hold values from 150 to 300
- moveouts: int32 [32, 16], replicated, may hold values from 0 to 63
- chan_mask: int32 [32, 3], P('parts'), parts along dimension 0, may hold values 0 or 1
- subnet: int32 [16], replicated, may hold values from 0 to 1
Outputs:
- network_stack: float32 [32, 2, 1536], P(('tmpl', 'sta'), None, ('parts', 'sub')), parts along dimension 2
There are 2 independent parts, one for each index of `parts`. A program takes and returns all parts, laid end to end along the dimension named above; an argument that names none is the same for every part. Nothing has to cross between parts.
All inputs are finite; a program needn't handle non-finite values.
Results may differ from a plain program's by a relative error of at most 0.0003.
Values may be sent and summed in bfloat16 or wider, within the bound.
A program may use at most 64 MiB of HBM per device.

v0:
```python
import functools

import jax
import jax.numpy as jnp
from jax import lax
from jax.experimental import pallas as pl
from jax.experimental.pallas import tpu as pltpu
from jax.sharding import PartitionSpec as P

REGIONS = 2
CHANNELS = 3
LANES = 128
GROUP = 16
F32 = jnp.float32
BF16 = jnp.bfloat16
NT_DIMS = (((1,), (1,)), ((), ()))


def ceil_div(a, b):
    return -(-a // b)


def each(count, body):
    if count <= 16:
        for i in range(count):
            body(i)
    else:
        lax.fori_loop(0, count, lambda i, c: (body(i), c)[1], 0)


def kernel(
    n_sta, n_own, share,
    traces_hbm, tail_hbm, templates_hbm, wins_hbm, lags_hbm, mask_hbm, subnet_hbm,
    out,
    tail, templates, wins, lags, mask, subnet,
    stage, send, recv, ebuf, tpad, wt, bt, acc, load_sem, send_sem, recv_sem,
):
    _, st_dev, t_dev = traces_hbm.shape
    halo = tail.shape[2]
    span = templates.shape[2]
    lag_bits = (halo - span).bit_length()
    own_blocks = t_dev // LANES
    u_blocks = ceil_div(t_dev + halo - span + 1, LANES)
    k_blocks = ceil_div(LANES + span - 1, LANES)
    width = k_blocks * LANES
    owners = GROUP // st_dev
    n_groups = n_own // owners
    everyone = 2 * n_own

    t_me = lax.axis_index("tmpl")
    a_me = lax.axis_index("sta")
    u_me = lax.axis_index("sub")
    own = t_me * n_sta + a_me
    flat = own * 2 + u_me

    def place(d):
        other = lax.rem(flat + d, everyone)
        return {"tmpl": other // (2 * n_sta), "sta": (other // 2) % n_sta, "sub": other % 2}

    pairs = [
        (traces_hbm, send.at[0]), (tail_hbm, tail), (templates_hbm, templates), (wins_hbm, wins),
        (lags_hbm, lags), (mask_hbm, mask), (subnet_hbm, subnet),
    ]
    loads = [pltpu.make_async_copy(a, b, load_sem.at[i]) for i, (a, b) in enumerate(pairs)]
    for load in loads:
        load.start()

    barrier = pltpu.get_barrier_semaphore()

    def greet(i):
        pl.semaphore_signal(barrier, inc=1, device_id=place(i + 1), device_id_type=pl.DeviceIdType.MESH)

    each(everyone - 1, greet)

    stage[...] = jnp.zeros_like(stage)
    tpad[...] = jnp.zeros_like(tpad)
    loads[0].wait()
    loads[1].wait()
    for c in range(CHANNELS):
        stage[c, :, pl.ds(0, halo)] = tail[c].astype(F32)
        main = send[0, c]
        recv[own, 0, c] = main
        send[1, c] = jnp.where(u_me == 1, main.astype(F32), stage[c]).astype(BF16)

    pl.semaphore_wait(barrier, everyone - 1)

    def outgoing(i):
        d = i + 1
        half = d % 2
        return pltpu.make_async_remote_copy(
            src_ref=send.at[half],
            dst_ref=recv.at[own, half],
            send_sem=send_sem.at[i],
            recv_sem=recv_sem.at[i],
            device_id=place(d),
            device_id_type=pl.DeviceIdType.MESH,
        )

    order = sorted(range(everyone - 1), key=lambda i: abs(i + 1 - n_own))
    if n_groups == 1:
        for i in order:
            outgoing(i).start()
    else:
        each(everyone - 1, lambda i: outgoing(i).start())

    for load in loads[2:]:
        load.wait()
    first = own * share

    def picked(values, at):
        lane = lax.broadcasted_iota(jnp.int32, values.shape, 1)
        return jnp.sum(jnp.where(lane == at, values, 0).astype(F32), axis=1, keepdims=True)

    row_at = lax.broadcasted_iota(jnp.int32, (LANES, width), 0)
    col_at = lax.broadcasted_iota(jnp.int32, (LANES, width), 1)
    apart = col_at - row_at
    floor_rows = []
    for k in range(share):
        win = picked(wins[...], first + k)
        floor_rows.append(jnp.broadcast_to(1e-05 * win, (1, LANES)))
        band = jnp.logical_and(apart >= 0, apart < win.astype(jnp.int32))
        bt[pl.ds(k * LANES, LANES), :] = jnp.where(band, 1.0, 0.0).astype(BF16)
    norm_rows = []
    for c in range(CHANNELS):
        tpad[c, :, pl.ds(0, span)] = templates[c].astype(F32)
        norms = []
        for k in range(share):
            taps = tpad[c, pl.ds(a_me * share + k, 1), :]
            power = jnp.sum(taps * taps, axis=1, keepdims=True)
            norms.append(jnp.broadcast_to(1.0 / jnp.sqrt(power + 1e-06), (1, LANES)))
            line = jnp.broadcast_to(taps, (LANES, width))
            slid = pltpu.roll(line, 0, 1, stride=1, stride_axis=0)
            wt[c, pl.ds(k * LANES, LANES), :] = slid.astype(BF16)
        norm_rows.append(jnp.concatenate(norms, axis=1))
    floor_row = jnp.concatenate(floor_rows, axis=1)

    lane_at = lax.broadcasted_iota(jnp.int32, (share * GROUP, LANES), 1)

    def prepare(group):
        base = group * GROUP
        rows = lags[pl.ds(base, GROUP), :]
        lag = jnp.concatenate([picked(rows, first + k) for k in range(share)], axis=0)
        lag = jnp.broadcast_to(lag.astype(jnp.int32), (share * GROUP, LANES))
        square = (GROUP, subnet.shape[1])
        here = lax.broadcasted_iota(jnp.int32, square, 1) == base + lax.broadcasted_iota(
            jnp.int32, square, 0
        )

        def column(row):
            spread_row = jnp.broadcast_to(row.astype(F32), square)
            return jnp.sum(jnp.where(here, spread_row, 0.0), axis=1, keepdims=True)

        region = jnp.broadcast_to(column(subnet[...]).astype(jnp.int32), (GROUP, LANES))
        open_ = [column(mask[pl.ds(c, 1), :]) for c in range(CHANNELS)]
        live = jnp.maximum(functools.reduce(jnp.add, open_), 1.0)
        return lag, region, [o / live for o in open_]

    def work(group, ready):
        lag, region, weight = ready
        for o in range(owners):
            for half in range(2):
                for c in range(CHANNELS):
                    block = recv[group * owners + o, half, c].astype(F32)
                    for n in range(own_blocks):
                        ebuf[c, half * own_blocks + n, pl.ds(o * st_dev, st_dev), :] = block[
                            :, n * LANES : (n + 1) * LANES
                        ]

        def spread(parts):
            empty = jnp.zeros_like(parts[0])
            parts = parts + [empty] * (u_blocks + k_blocks - 1 - len(parts))
            return jnp.concatenate(
                [jnp.concatenate(parts[j : j + u_blocks], axis=0) for j in range(k_blocks)], axis=1
            )

        corr = []
        squares = []
        for c in range(CHANNELS):
            wave = [ebuf[c, n] for n in range(2 * own_blocks)]
            corr.append(
                lax.dot_general(
                    spread([w.astype(BF16) for w in wave]), wt[c], NT_DIMS, preferred_element_type=F32
                )
            )
            high = [(w * w).astype(BF16) for w in wave]
            low = [(w * w - h.astype(F32)).astype(BF16) for w, h in zip(wave, high)]
            squares.append(spread(high))
            squares.append(spread(low))
        energy = lax.dot_general(
            jnp.concatenate(squares, axis=0), bt[...], NT_DIMS, preferred_element_type=F32
        )
        tall = u_blocks * GROUP
        coherent = None
        for c in range(CHANNELS):
            at = 2 * c * tall
            power = energy[at : at + tall] + energy[at + tall : at + 2 * tall]
            scale = jnp.concatenate([weight[c]] * u_blocks, axis=0)
            term = corr[c] * lax.rsqrt(power + floor_row) * (scale * norm_rows[c])
            coherent = term if coherent is None else coherent + term

        pieces = [
            jnp.concatenate(
                [
                    coherent[b * GROUP : (b + 1) * GROUP, k * LANES : (k + 1) * LANES]
                    for k in range(share)
                ],
                axis=0,
            )
            for b in range(u_blocks)
        ]
        for bit in range(lag_bits):
            step = 1 << bit
            turned = [pltpu.roll(p, LANES - step, 1) for p in pieces]
            stays = lane_at < LANES - step
            taken = (lax.shift_right_logical(lag, bit) & 1) == 1
            pieces = [
                jnp.where(
                    taken, jnp.where(stays, turned[b], turned[min(b + 1, u_blocks - 1)]), pieces[b]
                )
                for b in range(u_blocks)
            ]
        for k in range(share):
            for r in range(REGIONS):
                member = region == r
                total = jnp.concatenate(
                    [
                        jnp.sum(
                            jnp.where(member, pieces[n][k * GROUP : (k + 1) * GROUP], 0.0),
                            axis=0,
                            keepdims=True,
                        )
                        for n in range(own_blocks)
                    ],
                    axis=1,
                )
                if n_groups == 1:
                    out[k, pl.ds(r, 1), :] = total
                else:
                    acc[k, pl.ds(r, 1), :] += total

    if n_groups == 1:
        ready = prepare(0)
        each(everyone - 1, lambda i: outgoing(i).wait_recv())
        work(0, ready)
    else:
        acc[...] = jnp.zeros_like(acc)
        each(everyone - 1, lambda i: outgoing(i).wait_recv())

        def one(group, carry):
            work(group, prepare(group))
            return carry

        lax.fori_loop(0, n_groups, one, 0)
        out[...] = acc[...]
    each(everyone - 1, lambda i: outgoing(i).wait_send())


def shards(traces, trace_tail, templates, win_lengths, moveouts, chan_mask, subnet):
    n_tmpl = lax.axis_size("tmpl")
    n_sta = lax.axis_size("sta")
    n_own = n_tmpl * n_sta
    st_dev, _, t_dev = traces.shape
    share = templates.shape[0] // n_sta
    span = templates.shape[2]
    width = ceil_div(LANES + span - 1, LANES) * LANES
    block = (CHANNELS, st_dev, t_dev)
    operands = (
        jnp.transpose(traces, (1, 0, 2)),
        jnp.transpose(trace_tail, (1, 0, 2)),
        jnp.transpose(templates, (1, 0, 2)),
        win_lengths.reshape(1, -1),
        moveouts.T,
        chan_mask.T,
        subnet.reshape(1, -1),
    )
    return pl.pallas_call(
        functools.partial(kernel, n_sta, n_own, share),
        out_shape=jax.ShapeDtypeStruct((share, REGIONS, t_dev), F32),
        in_specs=[pl.BlockSpec(memory_space=pltpu.HBM)] * len(operands),
        out_specs=pl.BlockSpec(memory_space=pltpu.VMEM),
        scratch_shapes=[pltpu.VMEM(x.shape, x.dtype) for x in operands[1:]]
        + [
            pltpu.VMEM(block, F32),
            pltpu.VMEM((2,) + block, BF16),
            pltpu.VMEM((n_own, 2) + block, BF16),
            pltpu.VMEM((CHANNELS, 2 * t_dev // LANES, GROUP, LANES), F32),
            pltpu.VMEM((CHANNELS, templates.shape[0], width), F32),
            pltpu.VMEM((CHANNELS, share * LANES, width), BF16),
            pltpu.VMEM((share * LANES, width), BF16),
            pltpu.VMEM((share, REGIONS, t_dev), F32),
            pltpu.SemaphoreType.DMA((len(operands),)),
            pltpu.SemaphoreType.DMA((2 * n_own - 1,)),
            pltpu.SemaphoreType.DMA((2 * n_own - 1,)),
        ],
        compiler_params=pltpu.CompilerParams(
            collective_id=0, has_side_effects=True, vmem_limit_bytes=32 * 1024 * 1024
        ),
        name="matched_filter",
    )(*(pltpu.with_memory_space_constraint(x, pltpu.HBM) for x in operands))


def solution(mesh):
    in_specs = (
        P(("tmpl", "sta"), None, ("parts", "sub")),
        P(("tmpl", "sta"), None, "parts"),
        P("tmpl", None, None),
        P(),
        P(),
        P("parts", None),
        P(),
    )
    out_specs = P(("tmpl", "sta"), None, ("parts", "sub"))
    return jax.shard_map(shards, mesh=mesh, in_specs=in_specs, out_specs=out_specs, check_vma=False)
```

profile of v0, /device:TPU:0, one launch (start us, length us, event | category | flops | bytes accessed | tf_op | source)
XLA Modules:
  0.0 11.4 jit_solution(11411795457860635050)
XLA Ops:
  0.0 10.8 %matched_filter.1 = f32[4,2,384]{2,1,0:T(2,128)S(1)} custom-call(bf16[3,2,384]{2,1,0:T(2,128)(2,1)} %bitcast.9, bf16[3,2,363]{2,1,0:T(2,128)(2,1)} %bitcast.10, bf16[3,8,300]{2,1,0:T(8,128)(2,1)} %bitcast.7, s32[1,32]{1,0:T(1,128)} %bitcast.12, s32[16,32]{1,0:T(8,128)} %bitcast.8, s32[3,16]{1,0:T(4,128)} %bitcast.11, s32[1,16]{1,0:T(1,128)} %bitcast.13), custom_call_target="tpu_custom_call" | custom-call | tf_op jit(solution)/shard_map/matched_filter/pallas_call | solution.py:276
  10.8 0.6 %copy.9 = f32[4,2,384]{2,1,0:T(2,128)} copy(f32[4,2,384]{2,1,0:T(2,128)S(1)} %matched_filter.1) | data formatting | bytes 24576
where the time goes:
time: 11.5 us; the launch traced here: 11.4 us
  Pallas kernels  10.8 us (94%)
  local copies, waits for them, and re-layouts  0.6 us (5%)
    pallas_call x1, Pallas kernels, shards(): pl.pallas_call(functools.partial(kernel, n_sta, n_own, share), out_shape=...  10.8 us
    unnamed x1, local copies, waits for them, and re-layouts  0.6 us

commit v1 on v0

--- a/solution.py
+++ b/solution.py
@@ -13,7 +13,6 @@
 GROUP = 16
 F32 = jnp.float32
 BF16 = jnp.bfloat16
-NT_DIMS = (((1,), (1,)), ((), ()))
 
 
 def ceil_div(a, b):
@@ -33,7 +32,7 @@
     traces_hbm, tail_hbm, templates_hbm, wins_hbm, lags_hbm, mask_hbm, subnet_hbm,
     out,
     tail, templates, wins, lags, mask, subnet,
-    stage, send, recv, ebuf, tpad, wt, bt, acc, load_sem, send_sem, recv_sem,
+    stage, send, recv, ebuf, tpad, lines, wt, bt, acc, load_sem, send_sem, recv_sem,
 ):
     _, st_dev, t_dev = traces_hbm.shape
     halo = tail.shape[2]
@@ -111,27 +110,46 @@
         lane = lax.broadcasted_iota(jnp.int32, values.shape, 1)
         return jnp.sum(jnp.where(lane == at, values, 0).astype(F32), axis=1, keepdims=True)
 
-    row_at = lax.broadcasted_iota(jnp.int32, (LANES, width), 0)
-    col_at = lax.broadcasted_iota(jnp.int32, (LANES, width), 1)
-    apart = col_at - row_at
+    row_at = lax.broadcasted_iota(jnp.int32, (width, LANES), 0)
+    col_at = lax.broadcasted_iota(jnp.int32, (width, LANES), 1)
+    apart = row_at - col_at
     floor_rows = []
     for k in range(share):
         win = picked(wins[...], first + k)
         floor_rows.append(jnp.broadcast_to(1e-05 * win, (1, LANES)))
         band = jnp.logical_and(apart >= 0, apart < win.astype(jnp.int32))
-        bt[pl.ds(k * LANES, LANES), :] = jnp.where(band, 1.0, 0.0).astype(BF16)
+        bt[:, pl.ds(k * LANES, LANES)] = jnp.where(band, 1.0, 0.0).astype(BF16)
+    mirror = lax.broadcasted_iota(jnp.int32, (width, width), 0) + lax.broadcasted_iota(
+        jnp.int32, (width, width), 1
+    )
+    mirror = jnp.where(mirror == span - 1, 1.0, 0.0).astype(BF16)
+    k_dev = templates.shape[1]
+    for c in range(CHANNELS):
+        tpad[c, :, pl.ds(0, span)] = templates[c].astype(F32)
+    mirrored = jnp.dot(
+        jnp.concatenate([tpad[c] for c in range(CHANNELS)], axis=0).astype(BF16),
+        mirror,
+        preferred_element_type=F32,
+    )
     norm_rows = []
     for c in range(CHANNELS):
-        tpad[c, :, pl.ds(0, span)] = templates[c].astype(F32)
         norms = []
         for k in range(share):
             taps = tpad[c, pl.ds(a_me * share + k, 1), :]
             power = jnp.sum(taps * taps, axis=1, keepdims=True)
             norms.append(jnp.broadcast_to(1.0 / jnp.sqrt(power + 1e-06), (1, LANES)))
-            line = jnp.broadcast_to(taps, (LANES, width))
-            slid = pltpu.roll(line, 0, 1, stride=1, stride_axis=0)
-            wt[c, pl.ds(k * LANES, LANES), :] = slid.astype(BF16)
         norm_rows.append(jnp.concatenate(norms, axis=1))
+        for j in range(k_blocks):
+            turned = pltpu.roll(
+                mirrored[c * k_dev : (c + 1) * k_dev], (j * LANES - span + 1) % width, 1
+            )
+            lines[c, j] = jnp.concatenate([turned[:, :LANES], turned[:, width - LANES :]], axis=1)
+            for k in range(share):
+                line = lines[c, j, pl.ds(a_me * share + k, 1), :]
+                slid = pltpu.roll(
+                    jnp.broadcast_to(line, (LANES, 2 * LANES)), 0, 1, stride=1, stride_axis=0
+                )
+                wt[c, pl.ds(j * LANES, LANES), pl.ds(k * LANES, LANES)] = slid[:, :LANES].astype(BF16)
     floor_row = jnp.concatenate(floor_rows, axis=1)
 
     lane_at = lax.broadcasted_iota(jnp.int32, (share * GROUP, LANES), 1)
@@ -178,16 +196,14 @@
         for c in range(CHANNELS):
             wave = [ebuf[c, n] for n in range(2 * own_blocks)]
             corr.append(
-                lax.dot_general(
-                    spread([w.astype(BF16) for w in wave]), wt[c], NT_DIMS, preferred_element_type=F32
-                )
+                jnp.dot(spread([w.astype(BF16) for w in wave]), wt[c], preferred_element_type=F32)
             )
             high = [(w * w).astype(BF16) for w in wave]
             low = [(w * w - h.astype(F32)).astype(BF16) for w, h in zip(wave, high)]
             squares.append(spread(high))
             squares.append(spread(low))
-        energy = lax.dot_general(
-            jnp.concatenate(squares, axis=0), bt[...], NT_DIMS, preferred_element_type=F32
+        energy = jnp.dot(
+            jnp.concatenate(squares, axis=0), bt[...], preferred_element_type=F32
         )
         tall = u_blocks * GROUP
         coherent = None
@@ -285,8 +301,9 @@
             pltpu.VMEM((n_own, 2) + block, BF16),
             pltpu.VMEM((CHANNELS, 2 * t_dev // LANES, GROUP, LANES), F32),
             pltpu.VMEM((CHANNELS, templates.shape[0], width), F32),
-            pltpu.VMEM((CHANNELS, share * LANES, width), BF16),
-            pltpu.VMEM((share * LANES, width), BF16),
+            pltpu.VMEM((CHANNELS, width // LANES, templates.shape[0], 2 * LANES), F32),
+            pltpu.VMEM((CHANNELS, width, share * LANES), BF16),
+            pltpu.VMEM((width, share * LANES), BF16),
             pltpu.VMEM((share, REGIONS, t_dev), F32),
             pltpu.SemaphoreType.DMA((len(operands),)),
             pltpu.SemaphoreType.DMA((2 * n_own - 1,)),

time: 11.5 us -> 11.3 us (0.983)
  Pallas kernels: 10.8 us -> 10.5 us
    pallas_call x1, Pallas kernels: 10.8 us -> 10.5 us  [shards(): pl.pallas_call(functools.partial(kernel, n_sta, n_own, share), out_shape=...]
where the time goes in v1:
time: 11.3 us; the launch traced here: 11.1 us
  Pallas kernels  10.5 us (93%)
  local copies, waits for them, and re-layouts  0.6 us (5%)
    pallas_call x1, Pallas kernels, shards(): pl.pallas_call(functools.partial(kernel, n_sta, n_own, share), out_shape=...  10.5 us
    unnamed x1, local copies, waits for them, and re-layouts  0.6 us

profile of v1, /device:TPU:0, one launch (start us, length us, event | category | flops | bytes accessed | tf_op | source)
XLA Modules:
  0.0 11.1 jit_solution(16410723249744887492)
XLA Ops:
  0.0 10.5 %matched_filter.1 = f32[4,2,384]{2,1,0:T(2,128)S(1)} custom-call(bf16[3,2,384]{2,1,0:T(2,128)(2,1)} %bitcast.9, bf16[3,2,363]{2,1,0:T(2,128)(2,1)} %bitcast.10, bf16[3,8,300]{2,1,0:T(8,128)(2,1)} %bitcast.7, s32[1,32]{1,0:T(1,128)} %bitcast.12, s32[16,32]{1,0:T(8,128)} %bitcast.8, s32[3,16]{1,0:T(4,128)} %bitcast.11, s32[1,16]{1,0:T(1,128)} %bitcast.13), custom_call_target="tpu_custom_call" | custom-call | tf_op jit(solution)/shard_map/matched_filter/pallas_call | solution.py:292
  10.5 0.6 %copy.9 = f32[4,2,384]{2,1,0:T(2,128)} copy(f32[4,2,384]{2,1,0:T(2,128)S(1)} %matched_filter.1) | data formatting | bytes 24576

commit v2 on v1

--- a/solution.py
+++ b/solution.py
@@ -50,11 +50,17 @@
     a_me = lax.axis_index("sta")
     u_me = lax.axis_index("sub")
     own = t_me * n_sta + a_me
-    flat = own * 2 + u_me
 
     def place(d):
-        other = lax.rem(flat + d, everyone)
-        return {"tmpl": other // (2 * n_sta), "sta": (other // 2) % n_sta, "sub": other % 2}
+        if isinstance(d, int):
+            d_t, d_a, d_u = d // (2 * n_sta), d // 2 % n_sta, d % 2
+        else:
+            d_t, d_a, d_u = lax.div(d, 2 * n_sta), lax.rem(lax.div(d, 2), n_sta), lax.rem(d, 2)
+        return {
+            "tmpl": lax.rem(t_me + d_t, n_own // n_sta),
+            "sta": lax.rem(a_me + d_a, n_sta),
+            "sub": lax.rem(u_me + d_u, 2),
+        }
 
     pairs = [
         (traces_hbm, send.at[0]), (tail_hbm, tail), (templates_hbm, templates), (wins_hbm, wins),
@@ -78,29 +84,8 @@
     for c in range(CHANNELS):
         stage[c, :, pl.ds(0, halo)] = tail[c].astype(F32)
         main = send[0, c]
-        recv[own, 0, c] = main
+        recv[own * 2, c] = main
         send[1, c] = jnp.where(u_me == 1, main.astype(F32), stage[c]).astype(BF16)
-
-    pl.semaphore_wait(barrier, everyone - 1)
-
-    def outgoing(i):
-        d = i + 1
-        half = d % 2
-        return pltpu.make_async_remote_copy(
-            src_ref=send.at[half],
-            dst_ref=recv.at[own, half],
-            send_sem=send_sem.at[i],
-            recv_sem=recv_sem.at[i],
-            device_id=place(d),
-            device_id_type=pl.DeviceIdType.MESH,
-        )
-
-    order = sorted(range(everyone - 1), key=lambda i: abs(i + 1 - n_own))
-    if n_groups == 1:
-        for i in order:
-            outgoing(i).start()
-    else:
-        each(everyone - 1, lambda i: outgoing(i).start())
 
     for load in loads[2:]:
         load.wait()
@@ -119,6 +104,56 @@
         floor_rows.append(jnp.broadcast_to(1e-05 * win, (1, LANES)))
         band = jnp.logical_and(apart >= 0, apart < win.astype(jnp.int32))
         bt[:, pl.ds(k * LANES, LANES)] = jnp.where(band, 1.0, 0.0).astype(BF16)
+    floor_row = jnp.concatenate(floor_rows, axis=1)
+
+    lane_at = lax.broadcasted_iota(jnp.int32, (share * GROUP, LANES), 1)
+
+    def prepare(group):
+        base = group * GROUP
+        rows = lags[pl.ds(base, GROUP), :]
+        lag = jnp.concatenate([picked(rows, first + k) for k in range(share)], axis=0)
+        lag = jnp.broadcast_to(lag.astype(jnp.int32), (share * GROUP, LANES))
+        square = (GROUP, subnet.shape[1])
+        here = lax.broadcasted_iota(jnp.int32, square, 1) == base + lax.broadcasted_iota(
+            jnp.int32, square, 0
+        )
+
+        def column(row):
+            spread_row = jnp.broadcast_to(row.astype(F32), square)
+            return jnp.sum(jnp.where(here, spread_row, 0.0), axis=1, keepdims=True)
+
+        region = jnp.broadcast_to(column(subnet[...]).astype(jnp.int32), (GROUP, LANES))
+        open_ = [column(mask[pl.ds(c, 1), :]) for c in range(CHANNELS)]
+        live = jnp.maximum(functools.reduce(jnp.add, open_), 1.0)
+        return lag, region, [o / live for o in open_]
+
+    ready = prepare(0) if n_groups == 1 else None
+
+    pl.semaphore_wait(barrier, everyone - 1)
+
+    def outgoing(i):
+        d = i + 1
+        half = d % 2
+        return pltpu.make_async_remote_copy(
+            src_ref=send.at[half],
+            dst_ref=recv.at[own * 2 + half],
+            send_sem=send_sem,
+            recv_sem=recv_sem,
+            device_id=place(d),
+            device_id_type=pl.DeviceIdType.MESH,
+        )
+
+    blocks = recv.at[pl.ds(0, everyone - 1)]
+    arrived = pltpu.make_async_copy(blocks, blocks, recv_sem)
+    left = pltpu.make_async_copy(blocks, blocks, send_sem)
+
+    order = sorted(range(everyone - 1), key=lambda i: abs(i + 1 - n_own))
+    if n_groups == 1:
+        for i in order:
+            outgoing(i).start()
+    else:
+        each(everyone - 1, lambda i: outgoing(i).start())
+
     mirror = lax.broadcasted_iota(jnp.int32, (width, width), 0) + lax.broadcasted_iota(
         jnp.int32, (width, width), 1
     )
@@ -150,35 +185,13 @@
                     jnp.broadcast_to(line, (LANES, 2 * LANES)), 0, 1, stride=1, stride_axis=0
                 )
                 wt[c, pl.ds(j * LANES, LANES), pl.ds(k * LANES, LANES)] = slid[:, :LANES].astype(BF16)
-    floor_row = jnp.concatenate(floor_rows, axis=1)
-
-    lane_at = lax.broadcasted_iota(jnp.int32, (share * GROUP, LANES), 1)
-
-    def prepare(group):
-        base = group * GROUP
-        rows = lags[pl.ds(base, GROUP), :]
-        lag = jnp.concatenate([picked(rows, first + k) for k in range(share)], axis=0)
-        lag = jnp.broadcast_to(lag.astype(jnp.int32), (share * GROUP, LANES))
-        square = (GROUP, subnet.shape[1])
-        here = lax.broadcasted_iota(jnp.int32, square, 1) == base + lax.broadcasted_iota(
-            jnp.int32, square, 0
-        )
-
-        def column(row):
-            spread_row = jnp.broadcast_to(row.astype(F32), square)
-            return jnp.sum(jnp.where(here, spread_row, 0.0), axis=1, keepdims=True)
-
-        region = jnp.broadcast_to(column(subnet[...]).astype(jnp.int32), (GROUP, LANES))
-        open_ = [column(mask[pl.ds(c, 1), :]) for c in range(CHANNELS)]
-        live = jnp.maximum(functools.reduce(jnp.add, open_), 1.0)
-        return lag, region, [o / live for o in open_]
 
     def work(group, ready):
         lag, region, weight = ready
         for o in range(owners):
             for half in range(2):
                 for c in range(CHANNELS):
-                    block = recv[group * owners + o, half, c].astype(F32)
+                    block = recv[(group * owners + o) * 2 + half, c].astype(F32)
                     for n in range(own_blocks):
                         ebuf[c, half * own_blocks + n, pl.ds(o * st_dev, st_dev), :] = block[
                             :, n * LANES : (n + 1) * LANES
@@ -255,12 +268,11 @@
                     acc[k, pl.ds(r, 1), :] += total
 
     if n_groups == 1:
-        ready = prepare(0)
-        each(everyone - 1, lambda i: outgoing(i).wait_recv())
+        arrived.wait()
         work(0, ready)
     else:
         acc[...] = jnp.zeros_like(acc)
-        each(everyone - 1, lambda i: outgoing(i).wait_recv())
+        arrived.wait()
 
         def one(group, carry):
             work(group, prepare(group))
@@ -268,7 +280,7 @@
 
         lax.fori_loop(0, n_groups, one, 0)
         out[...] = acc[...]
-    each(everyone - 1, lambda i: outgoing(i).wait_send())
+    left.wait()
 
 
 def shards(traces, trace_tail, templates, win_lengths, moveouts, chan_mask, subnet):
@@ -298,7 +310,7 @@
         + [
             pltpu.VMEM(block, F32),
             pltpu.VMEM((2,) + block, BF16),
-            pltpu.VMEM((n_own, 2) + block, BF16),
+            pltpu.VMEM((2 * n_own,) + block, BF16),
             pltpu.VMEM((CHANNELS, 2 * t_dev // LANES, GROUP, LANES), F32),
             pltpu.VMEM((CHANNELS, templates.shape[0], width), F32),
             pltpu.VMEM((CHANNELS, width // LANES, templates.shape[0], 2 * LANES), F32),
@@ -306,8 +318,8 @@
             pltpu.VMEM((width, share * LANES), BF16),
             pltpu.VMEM((share, REGIONS, t_dev), F32),
             pltpu.SemaphoreType.DMA((len(operands),)),
-            pltpu.SemaphoreType.DMA((2 * n_own - 1,)),
-            pltpu.SemaphoreType.DMA((2 * n_own - 1,)),
+            pltpu.SemaphoreType.DMA,
+            pltpu.SemaphoreType.DMA,
         ],
         compiler_params=pltpu.CompilerParams(
             collective_id=0, has_side_effects=True, vmem_limit_bytes=32 * 1024 * 1024

time: 11.3 us -> 10.8 us (0.956)
  Pallas kernels: 10.5 us -> 10 us
    pallas_call x1, Pallas kernels: 10.5 us -> 10 us  [shards(): pl.pallas_call(functools.partial(kernel, n_sta, n_own, share), out_shape=...]
where the time goes in v2:
time: 10.8 us; the launch traced here: 10.6 us
  Pallas kernels  10 us (93%)
  local copies, waits for them, and re-layouts  0.6 us (6%)
    pallas_call x1, Pallas kernels, shards(): pl.pallas_call(functools.partial(kernel, n_sta, n_own, share), out_shape=...  10 us
    unnamed x1, local copies, waits for them, and re-layouts  0.6 us

profile of v2, /device:TPU:0, one launch (start us, length us, event | category | flops | bytes accessed | tf_op | source)
XLA Modules:
  0.0 10.6 jit_solution(10647118108410417565)
XLA Ops:
  0.0 10.0 %matched_filter.1 = f32[4,2,384]{2,1,0:T(2,128)S(1)} custom-call(bf16[3,2,384]{2,1,0:T(2,128)(2,1)} %bitcast.9, bf16[3,2,363]{2,1,0:T(2,128)(2,1)} %bitcast.10, bf16[3,8,300]{2,1,0:T(8,128)(2,1)} %bitcast.7, s32[1,32]{1,0:T(1,128)} %bitcast.12, s32[16,32]{1,0:T(8,128)} %bitcast.8, s32[3,16]{1,0:T(4,128)} %bitcast.11, s32[1,16]{1,0:T(1,128)} %bitcast.13), custom_call_target="tpu_custom_call" | custom-call | tf_op jit(solution)/shard_map/matched_filter/pallas_call | solution.py:304
  10.0 0.6 %copy.9 = f32[4,2,384]{2,1,0:T(2,128)} copy(f32[4,2,384]{2,1,0:T(2,128)S(1)} %matched_filter.1) | data formatting | bytes 24576

commit v3 on v2

--- a/solution.py
+++ b/solution.py
@@ -31,8 +31,8 @@
     n_sta, n_own, share,
     traces_hbm, tail_hbm, templates_hbm, wins_hbm, lags_hbm, mask_hbm, subnet_hbm,
     out,
-    tail, templates, wins, lags, mask, subnet,
-    stage, send, recv, ebuf, tpad, lines, wt, bt, acc, load_sem, send_sem, recv_sem,
+    traces, tail, templates, wins, lags, mask, subnet,
+    stage, send, recv, whole, tpad, lines, wt, bt, acc, load_sem, send_sem, recv_sem,
 ):
     _, st_dev, t_dev = traces_hbm.shape
     halo = tail.shape[2]
@@ -63,7 +63,7 @@
         }
 
     pairs = [
-        (traces_hbm, send.at[0]), (tail_hbm, tail), (templates_hbm, templates), (wins_hbm, wins),
+        (traces_hbm, traces), (tail_hbm, tail), (templates_hbm, templates), (wins_hbm, wins),
         (lags_hbm, lags), (mask_hbm, mask), (subnet_hbm, subnet),
     ]
     loads = [pltpu.make_async_copy(a, b, load_sem.at[i]) for i, (a, b) in enumerate(pairs)]
@@ -83,9 +83,12 @@
     loads[1].wait()
     for c in range(CHANNELS):
         stage[c, :, pl.ds(0, halo)] = tail[c].astype(F32)
-        main = send[0, c]
-        recv[own * 2, c] = main
-        send[1, c] = jnp.where(u_me == 1, main.astype(F32), stage[c]).astype(BF16)
+        for n in range(own_blocks):
+            lanes = pl.ds(n * LANES, LANES)
+            main = traces[c, :, lanes]
+            send[0, n, c] = main
+            send[1, n, c] = jnp.where(u_me == 1, main.astype(F32), stage[c, :, lanes]).astype(BF16)
+    pltpu.make_async_copy(send.at[0], recv.at[pl.ds(0, own_blocks), :, own], recv_sem).start()
 
     for load in loads[2:]:
         load.wait()
@@ -136,16 +139,15 @@
         half = d % 2
         return pltpu.make_async_remote_copy(
             src_ref=send.at[half],
-            dst_ref=recv.at[own * 2 + half],
+            dst_ref=recv.at[pl.ds(half * own_blocks, own_blocks), :, own],
             send_sem=send_sem,
             recv_sem=recv_sem,
             device_id=place(d),
             device_id_type=pl.DeviceIdType.MESH,
         )
 
-    blocks = recv.at[pl.ds(0, everyone - 1)]
-    arrived = pltpu.make_async_copy(blocks, blocks, recv_sem)
-    left = pltpu.make_async_copy(blocks, blocks, send_sem)
+    arrived = pltpu.make_async_copy(recv, recv, recv_sem)
+    left = pltpu.make_async_copy(whole, whole, send_sem)
 
     order = sorted(range(everyone - 1), key=lambda i: abs(i + 1 - n_own))
     if n_groups == 1:
@@ -188,14 +190,8 @@
 
     def work(group, ready):
         lag, region, weight = ready
-        for o in range(owners):
-            for half in range(2):
-                for c in range(CHANNELS):
-                    block = recv[(group * owners + o) * 2 + half, c].astype(F32)
-                    for n in range(own_blocks):
-                        ebuf[c, half * own_blocks + n, pl.ds(o * st_dev, st_dev), :] = block[
-                            :, n * LANES : (n + 1) * LANES
-                        ]
+        stations = recv.reshape(2 * own_blocks, CHANNELS, n_own * st_dev, LANES)
+        rows = pl.ds(group * GROUP, GROUP)
 
         def spread(parts):
             empty = jnp.zeros_like(parts[0])
@@ -207,10 +203,11 @@
         corr = []
         squares = []
         for c in range(CHANNELS):
-            wave = [ebuf[c, n] for n in range(2 * own_blocks)]
+            wave = [stations[n, c, rows, :] for n in range(2 * own_blocks)]
             corr.append(
-                jnp.dot(spread([w.astype(BF16) for w in wave]), wt[c], preferred_element_type=F32)
+                jnp.dot(spread(wave), wt[c], preferred_element_type=F32)
             )
+            wave = [w.astype(F32) for w in wave]
             high = [(w * w).astype(BF16) for w in wave]
             low = [(w * w - h.astype(F32)).astype(BF16) for w, h in zip(wave, high)]
             squares.append(spread(high))
@@ -291,7 +288,7 @@
     share = templates.shape[0] // n_sta
     span = templates.shape[2]
     width = ceil_div(LANES + span - 1, LANES) * LANES
-    block = (CHANNELS, st_dev, t_dev)
+    blocks = t_dev // LANES
     operands = (
         jnp.transpose(traces, (1, 0, 2)),
         jnp.transpose(trace_tail, (1, 0, 2)),
@@ -306,12 +303,12 @@
         out_shape=jax.ShapeDtypeStruct((share, REGIONS, t_dev), F32),
         in_specs=[pl.BlockSpec(memory_space=pltpu.HBM)] * len(operands),
         out_specs=pl.BlockSpec(memory_space=pltpu.VMEM),
-        scratch_shapes=[pltpu.VMEM(x.shape, x.dtype) for x in operands[1:]]
+        scratch_shapes=[pltpu.VMEM(x.shape, x.dtype) for x in operands]
         + [
-            pltpu.VMEM(block, F32),
-            pltpu.VMEM((2,) + block, BF16),
-            pltpu.VMEM((2 * n_own,) + block, BF16),
-            pltpu.VMEM((CHANNELS, 2 * t_dev // LANES, GROUP, LANES), F32),
+            pltpu.VMEM((CHANNELS, st_dev, t_dev), F32),
+            pltpu.VMEM((2, blocks, CHANNELS, st_dev, LANES), BF16),
+            pltpu.VMEM((2 * blocks, CHANNELS, n_own, st_dev, LANES), BF16),
+            pltpu.VMEM((2 * n_own - 1, blocks, CHANNELS, st_dev, LANES), BF16),
             pltpu.VMEM((CHANNELS, templates.shape[0], width), F32),
             pltpu.VMEM((CHANNELS, width // LANES, templates.shape[0], 2 * LANES), F32),
             pltpu.VMEM((CHANNELS, width, share * LANES), BF16),

time: 10.8 us -> 10.8 us (level)
  no operation moved by 1% of the time
where the time goes in v3:
time: 10.8 us; the launch traced here: 10.6 us
  Pallas kernels  9.98 us (92%)
  local copies, waits for them, and re-layouts  0.6 us (6%)
    pallas_call x1, Pallas kernels, shards(): pl.pallas_call(functools.partial(kernel, n_sta, n_own, share), out_shape=...  9.98 us
    unnamed x1, local copies, waits for them, and re-layouts  0.6 us

profile of v3, /device:TPU:0, one launch (start us, length us, event | category | flops | bytes accessed | tf_op | source)
XLA Modules:
  0.0 10.6 jit_solution(14051765598276657734)
XLA Ops:
  0.0 10.0 %matched_filter.1 = f32[4,2,384]{2,1,0:T(2,128)S(1)} custom-call(bf16[3,2,384]{2,1,0:T(2,128)(2,1)} %bitcast.9, bf16[3,2,363]{2,1,0:T(2,128)(2,1)} %bitcast.10, bf16[3,8,300]{2,1,0:T(8,128)(2,1)} %bitcast.7, s32[1,32]{1,0:T(1,128)} %bitcast.12, s32[16,32]{1,0:T(8,128)} %bitcast.8, s32[3,16]{1,0:T(4,128)} %bitcast.11, s32[1,16]{1,0:T(1,128)} %bitcast.13), custom_call_target="tpu_custom_call" | custom-call | tf_op jit(solution)/shard_map/matched_filter/pallas_call | solution.py:301
  10.0 0.6 %copy.9 = f32[4,2,384]{2,1,0:T(2,128)} copy(f32[4,2,384]{2,1,0:T(2,128)S(1)} %matched_filter.1) | data formatting | bytes 24576

commit v4 on v3

--- a/solution.py
+++ b/solution.py
@@ -13,6 +13,7 @@
 GROUP = 16
 F32 = jnp.float32
 BF16 = jnp.bfloat16
+NT_DIMS = (((1,), (1,)), ((), ()))
 
 
 def ceil_div(a, b):
@@ -32,7 +33,7 @@
     traces_hbm, tail_hbm, templates_hbm, wins_hbm, lags_hbm, mask_hbm, subnet_hbm,
     out,
     traces, tail, templates, wins, lags, mask, subnet,
-    stage, send, recv, whole, tpad, lines, wt, bt, acc, load_sem, send_sem, recv_sem,
+    stage, send, recv, whole, tpad, wt, bt, acc, load_sem, send_sem, recv_sem,
 ):
     _, st_dev, t_dev = traces_hbm.shape
     halo = tail.shape[2]
@@ -98,15 +99,15 @@
         lane = lax.broadcasted_iota(jnp.int32, values.shape, 1)
         return jnp.sum(jnp.where(lane == at, values, 0).astype(F32), axis=1, keepdims=True)
 
-    row_at = lax.broadcasted_iota(jnp.int32, (width, LANES), 0)
-    col_at = lax.broadcasted_iota(jnp.int32, (width, LANES), 1)
-    apart = row_at - col_at
+    row_at = lax.broadcasted_iota(jnp.int32, (LANES, width), 0)
+    col_at = lax.broadcasted_iota(jnp.int32, (LANES, width), 1)
+    apart = col_at - row_at
     floor_rows = []
     for k in range(share):
         win = picked(wins[...], first + k)
         floor_rows.append(jnp.broadcast_to(1e-05 * win, (1, LANES)))
         band = jnp.logical_and(apart >= 0, apart < win.astype(jnp.int32))
-        bt[:, pl.ds(k * LANES, LANES)] = jnp.where(band, 1.0, 0.0).astype(BF16)
+        bt[pl.ds(k * LANES, LANES), :] = jnp.where(band, 1.0, 0.0).astype(BF16)
     floor_row = jnp.concatenate(floor_rows, axis=1)
 
     lane_at = lax.broadcasted_iota(jnp.int32, (share * GROUP, LANES), 1)
@@ -156,37 +157,18 @@
     else:
         each(everyone - 1, lambda i: outgoing(i).start())
 
-    mirror = lax.broadcasted_iota(jnp.int32, (width, width), 0) + lax.broadcasted_iota(
-        jnp.int32, (width, width), 1
-    )
-    mirror = jnp.where(mirror == span - 1, 1.0, 0.0).astype(BF16)
-    k_dev = templates.shape[1]
+    norm_rows = []
     for c in range(CHANNELS):
         tpad[c, :, pl.ds(0, span)] = templates[c].astype(F32)
-    mirrored = jnp.dot(
-        jnp.concatenate([tpad[c] for c in range(CHANNELS)], axis=0).astype(BF16),
-        mirror,
-        preferred_element_type=F32,
-    )
-    norm_rows = []
-    for c in range(CHANNELS):
         norms = []
         for k in range(share):
             taps = tpad[c, pl.ds(a_me * share + k, 1), :]
             power = jnp.sum(taps * taps, axis=1, keepdims=True)
             norms.append(jnp.broadcast_to(1.0 / jnp.sqrt(power + 1e-06), (1, LANES)))
+            line = jnp.broadcast_to(taps, (LANES, width))
+            slid = pltpu.roll(line, 0, 1, stride=1, stride_axis=0)
+            wt[c, pl.ds(k * LANES, LANES), :] = slid.astype(BF16)
         norm_rows.append(jnp.concatenate(norms, axis=1))
-        for j in range(k_blocks):
-            turned = pltpu.roll(
-                mirrored[c * k_dev : (c + 1) * k_dev], (j * LANES - span + 1) % width, 1
-            )
-            lines[c, j] = jnp.concatenate([turned[:, :LANES], turned[:, width - LANES :]], axis=1)
-            for k in range(share):
-                line = lines[c, j, pl.ds(a_me * share + k, 1), :]
-                slid = pltpu.roll(
-                    jnp.broadcast_to(line, (LANES, 2 * LANES)), 0, 1, stride=1, stride_axis=0
-                )
-                wt[c, pl.ds(j * LANES, LANES), pl.ds(k * LANES, LANES)] = slid[:, :LANES].astype(BF16)
 
     def work(group, ready):
         lag, region, weight = ready
@@ -205,15 +187,15 @@
         for c in range(CHANNELS):
             wave = [stations[n, c, rows, :] for n in range(2 * own_blocks)]
             corr.append(
-                jnp.dot(spread(wave), wt[c], preferred_element_type=F32)
+                lax.dot_general(spread(wave), wt[c], NT_DIMS, preferred_element_type=F32)
             )
             wave = [w.astype(F32) for w in wave]
             high = [(w * w).astype(BF16) for w in wave]
             low = [(w * w - h.astype(F32)).astype(BF16) for w, h in zip(wave, high)]
             squares.append(spread(high))
             squares.append(spread(low))
-        energy = jnp.dot(
-            jnp.concatenate(squares, axis=0), bt[...], preferred_element_type=F32
+        energy = lax.dot_general(
+            jnp.concatenate(squares, axis=0), bt[...], NT_DIMS, preferred_element_type=F32
         )
         tall = u_blocks * GROUP
         coherent = None
@@ -310,9 +292,8 @@
             pltpu.VMEM((2 * blocks, CHANNELS, n_own, st_dev, LANES), BF16),
             pltpu.VMEM((2 * n_own - 1, blocks, CHANNELS, st_dev, LANES), BF16),
             pltpu.VMEM((CHANNELS, templates.shape[0], width), F32),
-            pltpu.VMEM((CHANNELS, width // LANES, templates.shape[0], 2 * LANES), F32),
-            pltpu.VMEM((CHANNELS, width, share * LANES), BF16),
-            pltpu.VMEM((width, share * LANES), BF16),
+            pltpu.VMEM((CHANNELS, share * LANES, width), BF16),
+            pltpu.VMEM((share * LANES, width), BF16),
             pltpu.VMEM((share, REGIONS, t_dev), F32),
             pltpu.SemaphoreType.DMA((len(operands),)),
             pltpu.SemaphoreType.DMA,

time: 10.8 us -> 10.9 us (level)
  Pallas kernels: 9.98 us -> 10.1 us
    pallas_call x1, Pallas kernels: 9.98 us -> 10.1 us  [shards(): pl.pallas_call(functools.partial(kernel, n_sta, n_own, share), out_shape=...]
where the time goes in v4:
time: 10.9 us; the launch traced here: 10.7 us
  Pallas kernels  10.1 us (93%)
  local copies, waits for them, and re-layouts  0.6 us (6%)
    pallas_call x1, Pallas kernels, shards(): pl.pallas_call(functools.partial(kernel, n_sta, n_own, share), out_shape=...  10.1 us
    unnamed x1, local copies, waits for them, and re-layouts  0.6 us

profile of v4, /device:TPU:0, one launch (start us, length us, event | category | flops | bytes accessed | tf_op | source)
XLA Modules:
  0.0 10.7 jit_solution(10153026699621799739)
XLA Ops:
  0.0 10.1 %matched_filter.1 = f32[4,2,384]{2,1,0:T(2,128)S(1)} custom-call(bf16[3,2,384]{2,1,0:T(2,128)(2,1)} %bitcast.9, bf16[3,2,363]{2,1,0:T(2,128)(2,1)} %bitcast.10, bf16[3,8,300]{2,1,0:T(8,128)(2,1)} %bitcast.7, s32[1,32]{1,0:T(1,128)} %bitcast.12, s32[16,32]{1,0:T(8,128)} %bitcast.8, s32[3,16]{1,0:T(4,128)} %bitcast.11, s32[1,16]{1,0:T(1,128)} %bitcast.13), custom_call_target="tpu_custom_call" | custom-call | tf_op jit(solution)/shard_map/matched_filter/pallas_call | solution.py:283
  10.1 0.6 %copy.9 = f32[4,2,384]{2,1,0:T(2,128)} copy(f32[4,2,384]{2,1,0:T(2,128)S(1)} %matched_filter.1) | data formatting | bytes 24576

commit v5 on v2

--- a/solution.py
+++ b/solution.py
@@ -11,6 +11,7 @@
 CHANNELS = 3
 LANES = 128
 GROUP = 16
+PAIR = 2
 F32 = jnp.float32
 BF16 = jnp.bfloat16
 
@@ -204,68 +205,74 @@
                 [jnp.concatenate(parts[j : j + u_blocks], axis=0) for j in range(k_blocks)], axis=1
             )
 
-        corr = []
+        waves = []
         squares = []
         for c in range(CHANNELS):
             wave = [ebuf[c, n] for n in range(2 * own_blocks)]
-            corr.append(
-                jnp.dot(spread([w.astype(BF16) for w in wave]), wt[c], preferred_element_type=F32)
-            )
+            waves.append(spread([w.astype(BF16) for w in wave]))
             high = [(w * w).astype(BF16) for w in wave]
             low = [(w * w - h.astype(F32)).astype(BF16) for w, h in zip(wave, high)]
             squares.append(spread(high))
             squares.append(spread(low))
-        energy = jnp.dot(
-            jnp.concatenate(squares, axis=0), bt[...], preferred_element_type=F32
-        )
+        squares = jnp.concatenate(squares, axis=0)
         tall = u_blocks * GROUP
-        coherent = None
-        for c in range(CHANNELS):
-            at = 2 * c * tall
-            power = energy[at : at + tall] + energy[at + tall : at + 2 * tall]
-            scale = jnp.concatenate([weight[c]] * u_blocks, axis=0)
-            term = corr[c] * lax.rsqrt(power + floor_row) * (scale * norm_rows[c])
-            coherent = term if coherent is None else coherent + term
-
-        pieces = [
-            jnp.concatenate(
-                [
-                    coherent[b * GROUP : (b + 1) * GROUP, k * LANES : (k + 1) * LANES]
-                    for k in range(share)
-                ],
-                axis=0,
-            )
-            for b in range(u_blocks)
-        ]
-        for bit in range(lag_bits):
-            step = 1 << bit
-            turned = [pltpu.roll(p, LANES - step, 1) for p in pieces]
-            stays = lane_at < LANES - step
-            taken = (lax.shift_right_logical(lag, bit) & 1) == 1
+        scales = [jnp.concatenate([weight[c]] * u_blocks, axis=0) for c in range(CHANNELS)]
+        for start in range(0, share, PAIR):
+            count = min(PAIR, share - start)
+            picks = slice(start * LANES, (start + count) * LANES)
+            energy = jnp.dot(squares, bt[:, picks], preferred_element_type=F32)
+            coherent = None
+            for c in range(CHANNELS):
+                at = 2 * c * tall
+                power = energy[at : at + tall] + energy[at + tall : at + 2 * tall]
+                corr = jnp.dot(waves[c], wt[c, :, picks], preferred_element_type=F32)
+                scale = scales[c] * norm_rows[c][:, picks]
+                term = corr * lax.rsqrt(power + floor_row[:, picks]) * scale
+                coherent = term if coherent is None else coherent + term
+            tops = slice(start * GROUP, (start + count) * GROUP)
+            lag_pair = lag[tops]
+            lanes = lane_at[tops]
             pieces = [
-                jnp.where(
-                    taken, jnp.where(stays, turned[b], turned[min(b + 1, u_blocks - 1)]), pieces[b]
+                jnp.concatenate(
+                    [
+                        coherent[b * GROUP : (b + 1) * GROUP, k * LANES : (k + 1) * LANES]
+                        for k in range(count)
+                    ],
+                    axis=0,
                 )
                 for b in range(u_blocks)
             ]
-        for k in range(share):
-            for r in range(REGIONS):
-                member = region == r
-                total = jnp.concatenate(
-                    [
-                        jnp.sum(
-                            jnp.where(member, pieces[n][k * GROUP : (k + 1) * GROUP], 0.0),
-                            axis=0,
-                            keepdims=True,
-                        )
-                        for n in range(own_blocks)
-                    ],
-                    axis=1,
-                )
-                if n_groups == 1:
-                    out[k, pl.ds(r, 1), :] = total
-                else:
-                    acc[k, pl.ds(r, 1), :] += total
+            for bit in range(lag_bits):
+                step = 1 << bit
+                turned = [pltpu.roll(p, LANES - step, 1) for p in pieces]
+                stays = lanes < LANES - step
+                taken = (lax.shift_right_logical(lag_pair, bit) & 1) == 1
+                pieces = [
+                    jnp.where(
+                        taken,
+                        jnp.where(stays, turned[b], turned[min(b + 1, u_blocks - 1)]),
+                        pieces[b],
+                    )
+                    for b in range(u_blocks)
+                ]
+            for k in range(count):
+                for r in range(REGIONS):
+                    member = region == r
+                    total = jnp.concatenate(
+                        [
+                            jnp.sum(
+                                jnp.where(member, pieces[n][k * GROUP : (k + 1) * GROUP], 0.0),
+                                axis=0,
+                                keepdims=True,
+                            )
+                            for n in range(own_blocks)
+                        ],
+                        axis=1,
+                    )
+                    if n_groups == 1:
+                        out[start + k, pl.ds(r, 1), :] = total
+                    else:
+                        acc[start + k, pl.ds(r, 1), :] += total
 
     if n_groups == 1:
         arrived.wait()

time: 10.8 us -> 10.7 us (level)
  no operation moved by 1% of the time
where the time goes in v5:
time: 10.7 us; the launch traced here: 10.5 us
  Pallas kernels  9.9 us (93%)
  local copies, waits for them, and re-layouts  0.6 us (6%)
    pallas_call x1, Pallas kernels, shards(): pl.pallas_call(functools.partial(kernel, n_sta, n_own, share), out_shape=...  9.9 us
    unnamed x1, local copies, waits for them, and re-layouts  0.6 us

profile of v5, /device:TPU:0, one launch (start us, length us, event | category | flops | bytes accessed | tf_op | source)
XLA Modules:
  0.0 10.5 jit_solution(6511084058064554920)
XLA Ops:
  0.0 9.9 %matched_filter.1 = f32[4,2,384]{2,1,0:T(2,128)S(1)} custom-call(bf16[3,2,384]{2,1,0:T(2,128)(2,1)} %bitcast.9, bf16[3,2,363]{2,1,0:T(2,128)(2,1)} %bitcast.10, bf16[3,8,300]{2,1,0:T(8,128)(2,1)} %bitcast.7, s32[1,32]{1,0:T(1,128)} %bitcast.12, s32[16,32]{1,0:T(8,128)} %bitcast.8, s32[3,16]{1,0:T(4,128)} %bitcast.11, s32[1,16]{1,0:T(1,128)} %bitcast.13), custom_call_target="tpu_custom_call" | custom-call | tf_op jit(solution)/shard_map/matched_filter/pallas_call | solution.py:311
  9.9 0.6 %copy.9 = f32[4,2,384]{2,1,0:T(2,128)} copy(f32[4,2,384]{2,1,0:T(2,128)S(1)} %matched_filter.1) | data formatting | bytes 24576

commit v6 on v5

--- a/solution.py
+++ b/solution.py
@@ -68,15 +68,19 @@
         (lags_hbm, lags), (mask_hbm, mask), (subnet_hbm, subnet),
     ]
     loads = [pltpu.make_async_copy(a, b, load_sem.at[i]) for i, (a, b) in enumerate(pairs)]
+    barrier = pltpu.get_barrier_semaphore()
+
+    def greet(i):
+        pl.semaphore_signal(barrier, inc=1, device_id=place(i + 1), device_id_type=pl.DeviceIdType.MESH)
+
+    order = sorted(range(everyone - 1), key=lambda i: abs(i + 1 - n_own))
+    if n_groups == 1:
+        for i in order:
+            greet(i)
+    else:
+        each(everyone - 1, greet)
     for load in loads:
         load.start()
-
-    barrier = pltpu.get_barrier_semaphore()
-
-    def greet(i):
-        pl.semaphore_signal(barrier, inc=1, device_id=place(i + 1), device_id_type=pl.DeviceIdType.MESH)
-
-    each(everyone - 1, greet)
 
     stage[...] = jnp.zeros_like(stage)
     tpad[...] = jnp.zeros_like(tpad)
@@ -87,48 +91,6 @@
         main = send[0, c]
         recv[own * 2, c] = main
         send[1, c] = jnp.where(u_me == 1, main.astype(F32), stage[c]).astype(BF16)
-
-    for load in loads[2:]:
-        load.wait()
-    first = own * share
-
-    def picked(values, at):
-        lane = lax.broadcasted_iota(jnp.int32, values.shape, 1)
-        return jnp.sum(jnp.where(lane == at, values, 0).astype(F32), axis=1, keepdims=True)
-
-    row_at = lax.broadcasted_iota(jnp.int32, (width, LANES), 0)
-    col_at = lax.broadcasted_iota(jnp.int32, (width, LANES), 1)
-    apart = row_at - col_at
-    floor_rows = []
-    for k in range(share):
-        win = picked(wins[...], first + k)
-        floor_rows.append(jnp.broadcast_to(1e-05 * win, (1, LANES)))
-        band = jnp.logical_and(apart >= 0, apart < win.astype(jnp.int32))
-        bt[:, pl.ds(k * LANES, LANES)] = jnp.where(band, 1.0, 0.0).astype(BF16)
-    floor_row = jnp.concatenate(floor_rows, axis=1)
-
-    lane_at = lax.broadcasted_iota(jnp.int32, (share * GROUP, LANES), 1)
-
-    def prepare(group):
-        base = group * GROUP
-        rows = lags[pl.ds(base, GROUP), :]
-        lag = jnp.concatenate([picked(rows, first + k) for k in range(share)], axis=0)
-        lag = jnp.broadcast_to(lag.astype(jnp.int32), (share * GROUP, LANES))
-        square = (GROUP, subnet.shape[1])
-        here = lax.broadcasted_iota(jnp.int32, square, 1) == base + lax.broadcasted_iota(
-            jnp.int32, square, 0
-        )
-
-        def column(row):
-            spread_row = jnp.broadcast_to(row.astype(F32), square)
-            return jnp.sum(jnp.where(here, spread_row, 0.0), axis=1, keepdims=True)
-
-        region = jnp.broadcast_to(column(subnet[...]).astype(jnp.int32), (GROUP, LANES))
-        open_ = [column(mask[pl.ds(c, 1), :]) for c in range(CHANNELS)]
-        live = jnp.maximum(functools.reduce(jnp.add, open_), 1.0)
-        return lag, region, [o / live for o in open_]
-
-    ready = prepare(0) if n_groups == 1 else None
 
     pl.semaphore_wait(barrier, everyone - 1)
 
@@ -148,12 +110,53 @@
     arrived = pltpu.make_async_copy(blocks, blocks, recv_sem)
     left = pltpu.make_async_copy(blocks, blocks, send_sem)
 
-    order = sorted(range(everyone - 1), key=lambda i: abs(i + 1 - n_own))
     if n_groups == 1:
         for i in order:
             outgoing(i).start()
     else:
         each(everyone - 1, lambda i: outgoing(i).start())
+
+    for load in loads[2:]:
+        load.wait()
+    first = own * share
+
+    def picked(values, at):
+        lane = lax.broadcasted_iota(jnp.int32, values.shape, 1)
+        return jnp.sum(jnp.where(lane == at, values, 0).astype(F32), axis=1, keepdims=True)
+
+    row_at = lax.broadcasted_iota(jnp.int32, (width, LANES), 0)
+    col_at = lax.broadcasted_iota(jnp.int32, (width, LANES), 1)
+    apart = row_at - col_at
+    floor_rows = []
+    for k in range(share):
+        win = picked(wins[...], first + k)
+        floor_rows.append(jnp.broadcast_to(1e-05 * win, (1, LANES)))
+        band = jnp.logical_and(apart >= 0, apart < win.astype(jnp.int32))
+        bt[:, pl.ds(k * LANES, LANES)] = jnp.where(band, 1.0, 0.0).astype(BF16)
+    floor_row = jnp.concatenate(floor_rows, axis=1)
+
+    lane_at = lax.broadcasted_iota(jnp.int32, (share * GROUP, LANES), 1)
+
+    def prepare(group):
+        base = group * GROUP
+        rows = lags[pl.ds(base, GROUP), :]
+        lag = jnp.concatenate([picked(rows, first + k) for k in range(share)], axis=0)
+        lag = jnp.broadcast_to(lag.astype(jnp.int32), (share * GROUP, LANES))
+        square = (GROUP, subnet.shape[1])
+        here = lax.broadcasted_iota(jnp.int32, square, 1) == base + lax.broadcasted_iota(
+            jnp.int32, square, 0
+        )
+
+        def column(row):
+            spread_row = jnp.broadcast_to(row.astype(F32), square)
+            return jnp.sum(jnp.where(here, spread_row, 0.0), axis=1, keepdims=True)
+
+        region = jnp.broadcast_to(column(subnet[...]).astype(jnp.int32), (GROUP, LANES))
+        open_ = [column(mask[pl.ds(c, 1), :]) for c in range(CHANNELS)]
+        live = jnp.maximum(functools.reduce(jnp.add, open_), 1.0)
+        return lag, region, [o / live for o in open_]
+
+    ready = prepare(0) if n_groups == 1 else None
 
     mirror = lax.broadcasted_iota(jnp.int32, (width, width), 0) + lax.broadcasted_iota(
         jnp.int32, (width, width), 1

time: 10.7 us -> 10.7 us (level)
  no operation moved by 1% of the time
where the time goes in v6:
time: 10.7 us; the launch traced here: 10.5 us
  Pallas kernels  9.93 us (93%)
  local copies, waits for them, and re-layouts  0.6 us (6%)
    pallas_call x1, Pallas kernels, shards(): pl.pallas_call(functools.partial(kernel, n_sta, n_own, share), out_shape=...  9.93 us
    unnamed x1, local copies, waits for them, and re-layouts  0.6 us

profile of v6, /device:TPU:0, one launch (start us, length us, event | category | flops | bytes accessed | tf_op | source)
XLA Modules:
  0.0 10.5 jit_solution(126784532026174539)
XLA Ops:
  0.0 9.9 %matched_filter.1 = f32[4,2,384]{2,1,0:T(2,128)S(1)} custom-call(bf16[3,2,384]{2,1,0:T(2,128)(2,1)} %bitcast.9, bf16[3,2,363]{2,1,0:T(2,128)(2,1)} %bitcast.10, bf16[3,8,300]{2,1,0:T(8,128)(2,1)} %bitcast.7, s32[1,32]{1,0:T(1,128)} %bitcast.12, s32[16,32]{1,0:T(8,128)} %bitcast.8, s32[3,16]{1,0:T(4,128)} %bitcast.11, s32[1,16]{1,0:T(1,128)} %bitcast.13), custom_call_target="tpu_custom_call" | custom-call | tf_op jit(solution)/shard_map/matched_filter/pallas_call | solution.py:314
  9.9 0.6 %copy.9 = f32[4,2,384]{2,1,0:T(2,128)} copy(f32[4,2,384]{2,1,0:T(2,128)S(1)} %matched_filter.1) | data formatting | bytes 24576

commit v7 on v6

--- a/solution.py
+++ b/solution.py
@@ -106,12 +106,16 @@
             device_id_type=pl.DeviceIdType.MESH,
         )
 
+    half_way = ceil_div(len(order), 2)
+    mixed = [i for pair in zip(order[:half_way], order[:half_way - 1:-1]) for i in pair]
+    mixed += order[half_way - 1 : half_way] if len(order) % 2 else []
+
     blocks = recv.at[pl.ds(0, everyone - 1)]
     arrived = pltpu.make_async_copy(blocks, blocks, recv_sem)
     left = pltpu.make_async_copy(blocks, blocks, send_sem)
 
     if n_groups == 1:
-        for i in order:
+        for i in mixed:
             outgoing(i).start()
     else:
         each(everyone - 1, lambda i: outgoing(i).start())

time: 10.7 us -> 10.9 us (1.019)
  Pallas kernels: 9.93 us -> 10.1 us
    pallas_call x1, Pallas kernels: 9.93 us -> 10.1 us  [shards(): pl.pallas_call(functools.partial(kernel, n_sta, n_own, share), out_shape=...]
where the time goes in v7:
time: 10.9 us; the launch traced here: 10.7 us
  Pallas kernels  10.1 us (93%)
  local copies, waits for them, and re-layouts  0.6 us (6%)
    pallas_call x1, Pallas kernels, shards(): pl.pallas_call(functools.partial(kernel, n_sta, n_own, share), out_shape=...  10.1 us
    unnamed x1, local copies, waits for them, and re-layouts  0.6 us

profile of v7, /device:TPU:0, one launch (start us, length us, event | category | flops | bytes accessed | tf_op | source)
XLA Modules:
  0.0 10.7 jit_solution(13898818392442074061)
XLA Ops:
  0.0 10.1 %matched_filter.1 = f32[4,2,384]{2,1,0:T(2,128)S(1)} custom-call(bf16[3,2,384]{2,1,0:T(2,128)(2,1)} %bitcast.9, bf16[3,2,363]{2,1,0:T(2,128)(2,1)} %bitcast.10, bf16[3,8,300]{2,1,0:T(8,128)(2,1)} %bitcast.7, s32[1,32]{1,0:T(1,128)} %bitcast.12, s32[16,32]{1,0:T(8,128)} %bitcast.8, s32[3,16]{1,0:T(4,128)} %bitcast.11, s32[1,16]{1,0:T(1,128)} %bitcast.13), custom_call_target="tpu_custom_call" | custom-call | tf_op jit(solution)/shard_map/matched_filter/pallas_call | solution.py:318
  10.1 0.6 %copy.9 = f32[4,2,384]{2,1,0:T(2,128)} copy(f32[4,2,384]{2,1,0:T(2,128)S(1)} %matched_filter.1) | data formatting | bytes 24576

commit v8 on v6

--- a/solution.py
+++ b/solution.py
@@ -32,8 +32,8 @@
     n_sta, n_own, share,
     traces_hbm, tail_hbm, templates_hbm, wins_hbm, lags_hbm, mask_hbm, subnet_hbm,
     out,
-    tail, templates, wins, lags, mask, subnet,
-    stage, send, recv, ebuf, tpad, lines, wt, bt, acc, load_sem, send_sem, recv_sem,
+    traces, tail, templates, wins, lags, mask, subnet,
+    stage, send, recv, whole, tpad, lines, wt, bt, acc, load_sem, send_sem, recv_sem,
 ):
     _, st_dev, t_dev = traces_hbm.shape
     halo = tail.shape[2]
@@ -64,7 +64,7 @@
         }
 
     pairs = [
-        (traces_hbm, send.at[0]), (tail_hbm, tail), (templates_hbm, templates), (wins_hbm, wins),
+        (traces_hbm, traces), (tail_hbm, tail), (templates_hbm, templates), (wins_hbm, wins),
         (lags_hbm, lags), (mask_hbm, mask), (subnet_hbm, subnet),
     ]
     loads = [pltpu.make_async_copy(a, b, load_sem.at[i]) for i, (a, b) in enumerate(pairs)]
@@ -88,9 +88,12 @@
     loads[1].wait()
     for c in range(CHANNELS):
         stage[c, :, pl.ds(0, halo)] = tail[c].astype(F32)
-        main = send[0, c]
-        recv[own * 2, c] = main
-        send[1, c] = jnp.where(u_me == 1, main.astype(F32), stage[c]).astype(BF16)
+        for n in range(own_blocks):
+            lanes = pl.ds(n * LANES, LANES)
+            main = traces[c, :, lanes]
+            send[0, n, c] = main
+            send[1, n, c] = jnp.where(u_me == 1, main.astype(F32), stage[c, :, lanes]).astype(BF16)
+    pltpu.make_async_copy(send.at[0], recv.at[pl.ds(0, own_blocks), :, own], recv_sem).start()
 
     pl.semaphore_wait(barrier, everyone - 1)
 
@@ -99,16 +102,15 @@
         half = d % 2
         return pltpu.make_async_remote_copy(
             src_ref=send.at[half],
-            dst_ref=recv.at[own * 2 + half],
+            dst_ref=recv.at[pl.ds(half * own_blocks, own_blocks), :, own],
             send_sem=send_sem,
             recv_sem=recv_sem,
             device_id=place(d),
             device_id_type=pl.DeviceIdType.MESH,
         )
 
-    blocks = recv.at[pl.ds(0, everyone - 1)]
-    arrived = pltpu.make_async_copy(blocks, blocks, recv_sem)
-    left = pltpu.make_async_copy(blocks, blocks, send_sem)
+    arrived = pltpu.make_async_copy(recv, recv, recv_sem)
+    left = pltpu.make_async_copy(whole, whole, send_sem)
 
     if n_groups == 1:
         for i in order:
@@ -192,14 +194,8 @@
 
     def work(group, ready):
         lag, region, weight = ready
-        for o in range(owners):
-            for half in range(2):
-                for c in range(CHANNELS):
-                    block = recv[(group * owners + o) * 2 + half, c].astype(F32)
-                    for n in range(own_blocks):
-                        ebuf[c, half * own_blocks + n, pl.ds(o * st_dev, st_dev), :] = block[
-                            :, n * LANES : (n + 1) * LANES
-                        ]
+        stations = recv.reshape(2 * own_blocks, CHANNELS, n_own * st_dev, LANES)
+        rows = pl.ds(group * GROUP, GROUP)
 
         def spread(parts):
             empty = jnp.zeros_like(parts[0])
@@ -211,8 +207,9 @@
         waves = []
         squares = []
         for c in range(CHANNELS):
-            wave = [ebuf[c, n] for n in range(2 * own_blocks)]
-            waves.append(spread([w.astype(BF16) for w in wave]))
+            wave = [stations[n, c, rows, :] for n in range(2 * own_blocks)]
+            waves.append(spread(wave))
+            wave = [w.astype(F32) for w in wave]
             high = [(w * w).astype(BF16) for w in wave]
             low = [(w * w - h.astype(F32)).astype(BF16) for w, h in zip(wave, high)]
             squares.append(spread(high))
@@ -301,7 +298,7 @@
     share = templates.shape[0] // n_sta
     span = templates.shape[2]
     width = ceil_div(LANES + span - 1, LANES) * LANES
-    block = (CHANNELS, st_dev, t_dev)
+    blocks = t_dev // LANES
     operands = (
         jnp.transpose(traces, (1, 0, 2)),
         jnp.transpose(trace_tail, (1, 0, 2)),
@@ -316,12 +313,12 @@
         out_shape=jax.ShapeDtypeStruct((share, REGIONS, t_dev), F32),
         in_specs=[pl.BlockSpec(memory_space=pltpu.HBM)] * len(operands),
         out_specs=pl.BlockSpec(memory_space=pltpu.VMEM),
-        scratch_shapes=[pltpu.VMEM(x.shape, x.dtype) for x in operands[1:]]
+        scratch_shapes=[pltpu.VMEM(x.shape, x.dtype) for x in operands]
         + [
-            pltpu.VMEM(block, F32),
-            pltpu.VMEM((2,) + block, BF16),
-            pltpu.VMEM((2 * n_own,) + block, BF16),
-            pltpu.VMEM((CHANNELS, 2 * t_dev // LANES, GROUP, LANES), F32),
+            pltpu.VMEM((CHANNELS, st_dev, t_dev), F32),
+            pltpu.VMEM((2, blocks, CHANNELS, st_dev, LANES), BF16),
+            pltpu.VMEM((2 * blocks, CHANNELS, n_own, st_dev, LANES), BF16),
+            pltpu.VMEM((2 * n_own - 1, blocks, CHANNELS, st_dev, LANES), BF16),
             pltpu.VMEM((CHANNELS, templates.shape[0], width), F32),
             pltpu.VMEM((CHANNELS, width // LANES, templates.shape[0], 2 * LANES), F32),
             pltpu.VMEM((CHANNELS, width, share * LANES), BF16),

time: 10.7 us -> 10.7 us (level)
  no operation moved by 1% of the time
where the time goes in v8:
time: 10.7 us; the launch traced here: 10.5 us
  Pallas kernels  9.94 us (93%)
  local copies, waits for them, and re-layouts  0.6 us (6%)
    pallas_call x1, Pallas kernels, shards(): pl.pallas_call(functools.partial(kernel, n_sta, n_own, share), out_shape=...  9.94 us
    unnamed x1, local copies, waits for them, and re-layouts  0.6 us

profile of v8, /device:TPU:0, one launch (start us, length us, event | category | flops | bytes accessed | tf_op | source)
XLA Modules:
  0.0 10.5 jit_solution(13107531778157819431)
XLA Ops:
  0.0 9.9 %matched_filter.1 = f32[4,2,384]{2,1,0:T(2,128)S(1)} custom-call(bf16[3,2,384]{2,1,0:T(2,128)(2,1)} %bitcast.9, bf16[3,2,363]{2,1,0:T(2,128)(2,1)} %bitcast.10, bf16[3,8,300]{2,1,0:T(8,128)(2,1)} %bitcast.7, s32[1,32]{1,0:T(1,128)} %bitcast.12, s32[16,32]{1,0:T(8,128)} %bitcast.8, s32[3,16]{1,0:T(4,128)} %bitcast.11, s32[1,16]{1,0:T(1,128)} %bitcast.13), custom_call_target="tpu_custom_call" | custom-call | tf_op jit(solution)/shard_map/matched_filter/pallas_call | solution.py:311
  9.9 0.6 %copy.9 = f32[4,2,384]{2,1,0:T(2,128)} copy(f32[4,2,384]{2,1,0:T(2,128)S(1)} %matched_filter.1) | data formatting | bytes 24576

commit v9 on v8

--- a/solution.py
+++ b/solution.py
@@ -274,6 +274,7 @@
                     else:
                         acc[start + k, pl.ds(r, 1), :] += total
 
+    left.wait()
     if n_groups == 1:
         arrived.wait()
         work(0, ready)
@@ -287,7 +288,6 @@
 
         lax.fori_loop(0, n_groups, one, 0)
         out[...] = acc[...]
-    left.wait()
 
 
 def shards(traces, trace_tail, templates, win_lengths, moveouts, chan_mask, subnet):

time: 10.7 us -> 10.7 us (level)
  no operation moved by 1% of the time
where the time goes in v9:
time: 10.7 us; the launch traced here: 10.5 us
  Pallas kernels  9.94 us (93%)
  local copies, waits for them, and re-layouts  0.6 us (6%)
    pallas_call x1, Pallas kernels, shards(): pl.pallas_call(functools.partial(kernel, n_sta, n_own, share), out_shape=...  9.94 us
    unnamed x1, local copies, waits for them, and re-layouts  0.6 us

profile of v9, /device:TPU:0, one launch (start us, length us, event | category | flops | bytes accessed | tf_op | source)
XLA Modules:
  0.0 10.5 jit_solution(14908302749146612679)
XLA Ops:
  0.0 9.9 %matched_filter.1 = f32[4,2,384]{2,1,0:T(2,128)S(1)} custom-call(bf16[3,2,384]{2,1,0:T(2,128)(2,1)} %bitcast.9, bf16[3,2,363]{2,1,0:T(2,128)(2,1)} %bitcast.10, bf16[3,8,300]{2,1,0:T(8,128)(2,1)} %bitcast.7, s32[1,32]{1,0:T(1,128)} %bitcast.12, s32[16,32]{1,0:T(8,128)} %bitcast.8, s32[3,16]{1,0:T(4,128)} %bitcast.11, s32[1,16]{1,0:T(1,128)} %bitcast.13), custom_call_target="tpu_custom_call" | custom-call | tf_op jit(solution)/shard_map/matched_filter/pallas_call | solution.py:311
  9.9 0.6 %copy.9 = f32[4,2,384]{2,1,0:T(2,128)} copy(f32[4,2,384]{2,1,0:T(2,128)S(1)} %matched_filter.1) | data formatting | bytes 24576
